TPU v7x, 32 devices: a whole 2x2x4 slice. The times are simulated.
32 devices in a mesh: case: 4 (over y, x), tile: 8 (over z, core).
Axes of the slice: x: 2, y: 2, z: 4, core: 2. Of those that a mesh axis runs over, the one named last changes fastest.
Arguments:
- forcing: bfloat16 [4, 128, 512, 128], P('case', 'tile'), may hold values from -6 to 6
- permeability: float32 [4, 128, 512], P('case', 'tile'), may hold values from 0.05 to 1
- merge_weights: int32 [4], P('case'), may hold values from 4 to 6
- start_codes: int32 [2, 256, 128], replicated, may hold values from -7 to 7
Outputs:
- basis: bfloat16 [4, 65536, 128], P('case', 'tile')
All inputs are finite; a program needn't handle non-finite values.
Results may differ from a plain program's by a relative error of at most 0.018.
Values may be sent and summed in bfloat16 or wider, within the bound.
A program may use at most 64 MiB of HBM per device.

v0:
```python
import functools
import math

import jax
import jax.numpy as jnp
from jax import lax
from jax.experimental import pallas as pl
from jax.experimental.pallas import tpu as pltpu
from jax.sharding import PartitionSpec as P

STEPS = 3
LEVELS = 2
PAD = 8
PANEL = 16
GROUP = 4
HIGHEST = lax.Precision.HIGHEST
MESH = pl.DeviceIdType.MESH
VMEM_BYTES = 60 * 2**20


def peers(axis, size):
    me = lax.axis_index(axis)
    return [{axis: lax.rem(me + k, size)} for k in range(size)]


def barrier(*axes):
    sem = pltpu.get_barrier_semaphore()
    count = 0
    for axis, size in axes:
        for device in peers(axis, size)[1:]:
            pl.semaphore_signal(sem, inc=1, device_id=device, device_id_type=MESH)
            count += 1
    pl.semaphore_wait(sem, count)


def remote(src, dst, send, recv, device):
    return pltpu.make_async_remote_copy(
        src_ref=src, dst_ref=dst, send_sem=send, recv_sem=recv, device_id=device, device_id_type=MESH
    )


def front_kernel(
    cases, tiles, f_ref, p_ref, weight_ref, s_ref, gram_ref,
    halo, p_ext, p_turned, u, wide_a, wide_b, out, flat, part, core_in, core_sum, case_in, acc, chip_in,
    halo_send, halo_recv, p_send, p_recv, s_send, s_recv,
    rs_send, rs_recv, cs_send, cs_recv, ts_send, ts_recv, tg_send, tg_recv, cg_send, cg_recv, rg_send, rg_recv,
):
    rows, ny, lanes = f_ref.shape
    ext = rows + 2 * STEPS
    quarter = rows // cases
    case, tile = lax.axis_index("case"), lax.axis_index("tile")
    case_peers, tile_peers = peers("case", cases), peers("tile", tiles)
    chunk = 128
    barrier(("case", cases), ("tile", tiles))

    back = remote(f_ref.at[pl.ds(0, STEPS)], halo.at[1], halo_send.at[0], halo_recv.at[1], {"tile": tile - 1})
    ahead = remote(f_ref.at[pl.ds(rows - STEPS, STEPS)], halo.at[0], halo_send.at[1], halo_recv.at[0], {"tile": tile + 1})

    p_back = remote(
        p_ref.at[pl.ds(0, PAD)], p_ext.at[pl.ds(PAD + rows, PAD)], p_send.at[0], p_recv.at[1], {"tile": tile - 1}
    )
    p_ahead = remote(
        p_ref.at[pl.ds(rows - PAD, PAD)], p_ext.at[pl.ds(0, PAD)], p_send.at[1], p_recv.at[0], {"tile": tile + 1}
    )

    @pl.when(tile > 0)
    def _():
        p_back.start()
        back.start()

    @pl.when(tile < tiles - 1)
    def _():
        p_ahead.start()
        ahead.start()

    @pl.when(tile == 0)
    def _():
        p_ext[0:PAD] = jnp.zeros((PAD, ny), jnp.float32)

    @pl.when(tile == tiles - 1)
    def _():
        p_ext[PAD + rows : 2 * PAD + rows] = jnp.zeros((PAD, ny), jnp.float32)

    p_ext[PAD : PAD + rows] = p_ref[...]
    p_ext[2 * PAD + rows :] = jnp.zeros((lanes - 2 * PAD - rows, ny), jnp.float32)
    p_turned[0:PAD] = jnp.zeros((PAD, lanes), jnp.float32)
    p_turned[PAD + ny :] = jnp.zeros((PAD, lanes), jnp.float32)

    @pl.loop(0, ext)
    def _(r):
        zeros = jnp.zeros((PAD, lanes), jnp.float32)
        for at in (pl.ds(0, PAD), pl.ds(PAD + ny, PAD)):
            wide_a[r, at] = zeros
            for slot in range(STEPS):
                u[slot, r, at] = zeros

    @pl.when(tile > 0)
    def _():
        p_back.wait_send()
        p_ahead.wait_recv()

    @pl.when(tile < tiles - 1)
    def _():
        p_ahead.wait_send()
        p_back.wait_recv()

    for y in range(0, ny, lanes):
        p_turned[pl.ds(PAD + y, lanes)] = p_ext[:, y : y + lanes].T
    for y in range(0, ny, 64):
        mid = p_turned[pl.ds(PAD + y, 64)]
        around = p_turned[pl.ds(PAD + y + 1, 64)] + p_turned[pl.ds(PAD + y - 1, 64)]
        around = around + (pltpu.roll(mid, 1, 1) + pltpu.roll(mid, lanes - 1, 1))
        col_a = 0.12 * mid
        col_b = 1.0 - 0.12 * (4.0 * mid + around)
        for r in range(ext):
            at = r + PAD - STEPS
            wide_a[r, pl.ds(PAD + y, 64)] = jnp.broadcast_to(col_a[:, at : at + 1], (64, lanes))
            wide_b[r, pl.ds(y, 64)] = jnp.broadcast_to(col_b[:, at : at + 1], (64, lanes))

    def take(r, load):
        for y in range(0, ny, chunk):
            u[0, r, pl.ds(PAD + y, chunk)] = load(y).astype(jnp.float32)

    @pl.loop(0, rows)
    def _(r):
        take(r + STEPS, lambda y: f_ref[r, pl.ds(y, chunk)])

    @pl.when(tile > 0)
    def _():
        back.wait_send()
        ahead.wait_recv()

    @pl.when(tile < tiles - 1)
    def _():
        ahead.wait_send()
        back.wait_recv()

    @pl.when(tile == 0)
    def _():
        halo[0] = jnp.zeros((STEPS, ny, lanes), halo.dtype)

    @pl.when(tile == tiles - 1)
    def _():
        halo[1] = jnp.zeros((STEPS, ny, lanes), halo.dtype)

    @pl.loop(0, STEPS)
    def _(r):
        take(r, lambda y: halo[0, r, pl.ds(y, chunk)])
        take(r + STEPS + rows, lambda y: halo[1, r, pl.ds(y, chunk)])

    def stepped(src, r, y):
        at = pl.ds(PAD + y, chunk)
        sides = (r + 1, at), (r - 1, at), (r, pl.ds(PAD + y + 1, chunk)), (r, pl.ds(PAD + y - 1, chunk))
        coef = wide_a[r, at]
        value = wide_b[r, pl.ds(y, chunk)] * u[src, r, at]
        for i, j in sides:
            value = value + (coef + wide_a[i, j]) * u[src, i, j]
        return value

    def advance(step, low, high):
        def one(r, _):
            inside = ((r >= STEPS) | (tile > 0)) & ((r < STEPS + rows) | (tile < tiles - 1))
            mask = jnp.where(inside, 1.0, 0.0)
            for y in range(0, ny, chunk):
                u[step + 1, r, pl.ds(PAD + y, chunk)] = stepped(step, r, y) * mask
            return 0

        lax.fori_loop(low, high, one, 0)

    weight = jnp.sqrt(jnp.full((1, lanes), weight_ref[0].astype(jnp.float32)))
    copies = []
    for k in [k for k in range(cases) if k] + [0]:
        turn = lax.rem(case + k, cases)
        first = turn * quarter
        for step in range(STEPS - 1):
            reach = STEPS - 1 - step
            low = -reach if k == 1 else jnp.where(turn == 0, -reach, reach)
            advance(step, first + STEPS + low, first + STEPS + quarter + reach)

        @pl.loop(0, quarter)
        def _(i):
            for y in range(0, ny, chunk):
                value = (stepped(STEPS - 1, first + i + STEPS, y) * weight).astype(jnp.bfloat16)
                if k:
                    out[k, i, pl.ds(y, chunk)] = value
                else:
                    s_ref[case, i, pl.ds(y, chunk)] = value

        if k:
            copy = remote(out.at[k], s_ref.at[case], s_send.at[k], s_recv.at[k], case_peers[k])
            copy.start()
            copies.append(copy)
    for copy in copies:
        copy.wait()

    block = 0
    snaps = [s_ref[g].reshape(quarter * ny, lanes) for g in range(cases)]
    for g in range(cases):
        right = jnp.concatenate(snaps[g:], 1)
        terms = lax.dot_general(snaps[g], right, (((0,), (0,)), ((), ())), preferred_element_type=jnp.float32)
        for h in range(cases - g):
            flat[block * lanes : (block + 1) * lanes, :] = terms[:, h * lanes : (h + 1) * lanes]
            block += 1
    half, share = part.shape[2:4]
    for i in range(2 * cases * half):
        part[i // (cases * half), i // half % cases, i % half] = flat[i * share : (i + 1) * share, :]

    def exchange(devices, source, target, send, recv):
        started = [remote(source(k), target(k), send.at[k], recv.at[k], devices[k]) for k in range(1, len(devices))]
        for copy in started:
            copy.start()
        for copy in started:
            copy.wait()

    core, chip = lax.rem(tile, 2), lax.div(tile, 2)
    core_peers = [{"tile": tile}, {"tile": chip * 2 + 1 - core}]
    chip_peers = [{"tile": lax.rem(chip + k, half) * 2 + core} for k in range(half)]
    exchange(core_peers, lambda k: part.at[1 - core], lambda k: core_in, rs_send, rs_recv)
    core_sum[...] = part[core] + core_in[...]
    exchange(
        case_peers, lambda k: core_sum.at[lax.rem(case + k, cases)], lambda k: case_in.at[k], cs_send, cs_recv
    )
    total = core_sum[case]
    for k in range(1, cases):
        total = total + case_in[k]
    acc[...] = total
    exchange(
        chip_peers, lambda k: acc.at[lax.rem(chip + k, half)], lambda k: chip_in.at[k], ts_send, ts_recv
    )
    total = acc[chip]
    for k in range(1, half):
        total = total + chip_in[k]
    gram_ref[core, case, chip] = total
    mine = gram_ref.at[core, case, chip]
    exchange(chip_peers, lambda k: mine, lambda k: mine, tg_send, tg_recv)
    ours = gram_ref.at[core, case]
    exchange(case_peers, lambda k: ours, lambda k: ours, cg_send, cg_recv)
    exchange(core_peers, lambda k: gram_ref.at[core], lambda k: gram_ref.at[core], rg_send, rg_recv)


def front(cases, tiles, forcing, permeability, merge_weights):
    rows, ny, lanes = forcing.shape
    ext, quarter = rows + 2 * STEPS, rows // cases
    total = cases * (cases + 1) // 2 * lanes
    half = tiles // 2
    share = total // (2 * cases * half)
    f32, bf16 = jnp.float32, jnp.bfloat16
    vmem = pl.BlockSpec(memory_space=pltpu.VMEM)
    dma = pltpu.SemaphoreType.DMA
    return pl.pallas_call(
        functools.partial(front_kernel, cases, tiles),
        out_shape=(
            jax.ShapeDtypeStruct((cases, quarter, ny, lanes), bf16),
            jax.ShapeDtypeStruct((2, cases, half, share, lanes), f32),
        ),
        in_specs=[vmem, vmem, pl.BlockSpec(memory_space=pltpu.SMEM)],
        out_specs=(vmem, vmem),
        scratch_shapes=[
            pltpu.VMEM((2, STEPS, ny, lanes), bf16),
            pltpu.VMEM((lanes, ny), f32),
            pltpu.VMEM((ny + 2 * PAD, lanes), f32),
            pltpu.VMEM((STEPS, ext, ny + 2 * PAD, lanes), f32),
            pltpu.VMEM((ext, ny + 2 * PAD, lanes), f32),
            pltpu.VMEM((ext, ny, lanes), f32),
            pltpu.VMEM((cases, quarter, ny, lanes), bf16),
            pltpu.VMEM((total, lanes), f32),
            pltpu.VMEM((2, cases, half, share, lanes), f32),
            pltpu.VMEM((cases, half, share, lanes), f32),
            pltpu.VMEM((cases, half, share, lanes), f32),
            pltpu.VMEM((cases, half, share, lanes), f32),
            pltpu.VMEM((half, share, lanes), f32),
            pltpu.VMEM((half, share, lanes), f32),
            dma((2,)), dma((2,)),
            dma((2,)), dma((2,)),
            dma((cases,)), dma((cases,)),
            dma((2,)), dma((2,)),
            dma((cases,)), dma((cases,)),
            dma((half,)), dma((half,)),
            dma((half,)), dma((half,)),
            dma((cases,)), dma((cases,)),
            dma((2,)), dma((2,)),
        ],
        compiler_params=pltpu.CompilerParams(collective_id=0, has_side_effects=True, vmem_limit_bytes=VMEM_BYTES),
    )(forcing, permeability, merge_weights)


def dot(left, right):
    return jnp.dot(left, right, precision=HIGHEST, preferred_element_type=jnp.float32)


def dot_rows(left, right):
    return lax.dot_general(
        left, right, (((0,), (0,)), ((), ())), precision=HIGHEST, preferred_element_type=jnp.float32
    )


def inverse_factors(work, inners):
    count, size = len(inners), inners[0].shape[0]
    eye = (
        lax.broadcasted_iota(jnp.int32, (size, size), 0) == lax.broadcasted_iota(jnp.int32, (size, size), 1)
    ).astype(jnp.float32)
    for b in range(count):
        work[b, :, :size] = inners[b]
        work[b, :, size:] = eye
    shape = (count, PANEL, size)
    index = lax.broadcasted_iota(jnp.int32, shape, 1)
    for top in range(0, size, PANEL):
        left = work[:count, top : top + PANEL, :size]
        right = work[:count, top : top + PANEL, size:]
        scale = jnp.ones(shape, jnp.float32)
        for group in range(0, PANEL, GROUP):
            at = top + group
            columns = [jnp.broadcast_to(left[:, :, at + j : at + j + 1], shape) for j in range(GROUP)]
            for j in range(GROUP):
                i = group + j
                root = lax.rsqrt(columns[j][:, i : i + 1, :])
                scale = jnp.where(index == i, root, scale)
                factor = jnp.where(index > i, columns[j] * (root * root), 0.0)
                for m in range(j + 1, GROUP):
                    columns[m] = columns[m] - factor * columns[m][:, i : i + 1, :]
                left = left - factor * left[:, i : i + 1, :]
                right = right - factor * right[:, i : i + 1, :]
        panel = jnp.concatenate([left * scale, right * scale], 2)
        work[:count, top : top + PANEL, :] = panel
        below = top + PANEL
        if below < size:
            for b in range(count):
                lead = panel[b][:, :size]
                update = dot_rows(lead, panel[b])
                work[b, below:, :] = work[b, below:, :] - update[below:, :]
    return [work[b, :, size:] for b in range(count)]


def solve_kernel(cells, gram_ref, code_ref, out_ref, full, work):
    cases, lanes = out_ref.shape[0], out_ref.shape[2]
    case = lax.axis_index("case")
    block = 0
    for g in range(cases):
        for h in range(g, cases):
            value = gram_ref[block]
            full[g, h] = value
            if h != g:
                full[h, g] = value.T
            block += 1
    groups = [jnp.bitwise_xor(case, g) for g in range(cases)]
    grams = {(g, h): full[groups[g], groups[h]] for g in range(cases) for h in range(cases)}
    chains = [[0]]
    for level in range(LEVELS - 1, 0, -1):
        chains.insert(0, sorted({c ^ bit for c in chains[0] for bit in (0, 2**level)}))

    def joined(left, right):
        return jnp.concatenate([jnp.concatenate([grams[g, h] for h in right], 1) for g in left], 0)

    bases = {c: ([c], None) for c in range(cases)}
    for level in range(LEVELS):
        crossed = {}

        def cross(g, h):
            if (h, g) in crossed:
                return crossed[h, g].T
            if (g, h) not in crossed:
                value = dot(joined(bases[g][0], bases[h][0]), bases[h][1])
                crossed[g, h] = dot_rows(bases[g][1], value)
            return crossed[g, h]

        start = code_ref[level].astype(jnp.float32)
        coeffs, inners = [], []
        for c in chains[level]:
            pair = (c, c ^ 2**level)
            if level == 0:
                gram = joined(pair, pair)
            else:
                rows = []
                for g in pair:
                    parts = [cross(g, h) for h in pair]
                    rows.append(jnp.concatenate(parts, 1))
                gram = jnp.concatenate(rows, 0)
            first = dot(gram, start) / cells
            second = dot(gram, first) / cells
            coeff = second.astype(jnp.bfloat16).astype(jnp.float32)
            coeffs.append(coeff)
            inners.append(dot_rows(coeff, dot(gram, coeff)))
        inverses = inverse_factors(work, inners)
        updated = {}
        for i, c in enumerate(chains[level]):
            p = c ^ 2**level
            turned = lax.dot_general(
                coeffs[i], inverses[i], (((1,), (1,)), ((), ())), precision=HIGHEST, preferred_element_type=jnp.float32
            ) * math.sqrt(cells)
            if level == 0:
                updated[c] = ([c, p], turned)
            else:
                head, tail = turned[:lanes], turned[lanes:]
                updated[c] = (
                    bases[c][0] + bases[p][0],
                    jnp.concatenate([dot(bases[c][1], head), dot(bases[p][1], tail)], 0),
                )
        bases = updated
    members, matrix = bases[0]
    for i, g in enumerate(members):
        out_ref[groups[g]] = matrix[i * lanes : (i + 1) * lanes].astype(out_ref.dtype)


def solve(cases, cells, grams, codes):
    lanes = grams.shape[-1]
    vmem = pl.BlockSpec(memory_space=pltpu.VMEM)
    return pl.pallas_call(
        functools.partial(solve_kernel, cells),
        out_shape=jax.ShapeDtypeStruct((cases, lanes, lanes), jnp.bfloat16),
        in_specs=[vmem] * 2,
        out_specs=vmem,
        scratch_shapes=[
            pltpu.VMEM((cases, cases, lanes, lanes), jnp.float32),
            pltpu.VMEM((cases, lanes, 2 * lanes), jnp.float32),
        ],
        compiler_params=pltpu.CompilerParams(vmem_limit_bytes=VMEM_BYTES),
    )(grams, codes)


def back_kernel(cases, s_ref, m_ref, out_ref, buffer, m_in, send, recv, m_send, m_recv):
    case = lax.axis_index("case")
    case_peers = peers("case", cases)
    cells = s_ref.shape[1]
    pieces = send.shape[1]
    chunk = cells // pieces
    barrier(("case", cases))
    copies = [remote(m_ref, m_in.at[k], m_send.at[k], m_recv.at[k], case_peers[k]) for k in range(1, cases)]
    for copy in copies:
        copy.start()

    def product(i, matrix):
        at = pl.ds(i * chunk, chunk)
        left = jnp.concatenate([s_ref[g, at, :] for g in range(cases)], 1)
        return jnp.dot(left, matrix, preferred_element_type=jnp.float32).astype(out_ref.dtype)

    for i in range(pieces):
        out_ref[case, pl.ds(i * chunk, chunk), :] = product(i, m_ref[...])
    for copy in copies:
        copy.wait()
    copies = []
    for i in range(pieces):
        at = pl.ds(i * chunk, chunk)
        for k in range(1, cases):
            buffer[k, at, :] = product(i, m_in[cases - k])
            copy = remote(buffer.at[k, at], out_ref.at[case, at], send.at[k, i], recv.at[k, i], case_peers[k])
            copy.start()
            copies.append(copy)
    for copy in copies:
        copy.wait()


def back(cases, snaps, matrices):
    vmem = pl.BlockSpec(memory_space=pltpu.VMEM)
    return pl.pallas_call(
        functools.partial(back_kernel, cases),
        out_shape=jax.ShapeDtypeStruct(snaps.shape, jnp.bfloat16),
        in_specs=[vmem] * 2,
        out_specs=vmem,
        scratch_shapes=[
            pltpu.VMEM(snaps.shape, jnp.bfloat16),
            pltpu.VMEM((cases,) + matrices.shape, jnp.bfloat16),
            pltpu.SemaphoreType.DMA((cases, 4)),
            pltpu.SemaphoreType.DMA((cases, 4)),
            pltpu.SemaphoreType.DMA((cases,)),
            pltpu.SemaphoreType.DMA((cases,)),
        ],
        compiler_params=pltpu.CompilerParams(collective_id=1, has_side_effects=True, vmem_limit_bytes=VMEM_BYTES),
    )(snaps, matrices)


def per_device(cases, tiles, forcing, permeability, merge_weights, start_codes):
    _, rows, ny, lanes = forcing.shape
    snaps, grams = front(cases, tiles, forcing[0], permeability[0], merge_weights)
    cells = rows * tiles * ny
    matrices = solve(cases, cells, grams.reshape(-1, lanes, lanes), start_codes)
    basis = back(cases, snaps.reshape(cases, -1, lanes), matrices.reshape(-1, lanes))
    return basis.reshape(1, -1, lanes)


def solution(mesh):
    placed = (P("case", "tile", None, None), P("case", "tile", None), P("case"), P())
    return jax.shard_map(
        functools.partial(per_device, mesh.shape["case"], mesh.shape["tile"]),
        mesh=mesh, in_specs=placed, out_specs=P("case", "tile", None), check_vma=False,
    )
```

profile of v0, /device:TPU:0, one launch (start us, length us, event | category | flops | bytes accessed | tf_op | source)
XLA Modules:
  0.0 135.7 jit_solution(9881112231002006858)
XLA Ops:
  0.7 68.1 %shard_map.46 = (bf16[4,4,512,128]{3,2,1,0:T(8,128)(2,1)}, f32[2,4,4,40,128]{4,3,2,1,0:T(8,128)}) custom-call(bf16[16,512,128]{2,1,0:T(8,128)(2,1)} %bitcast.7, f32[16,512]{1,0:T(8,128)} %bitcast.11, s32[1]{0:T(128)S(6)} %copy.6.weight_ref), custom_call_target="tpu_custom_call" | custom-call | tf_op jit(solution)/shard_map/pallas_call | solution.py:250
  68.8 25.5 %shard_map.47 = bf16[4,128,128]{2,1,0:T(8,128)(2,1)} custom-call(f32[10,128,128]{2,1,0:T(8,128)} %bitcast.9, s32[2,256,128]{2,1,0:T(8,128)} %code_ref.1), custom_call_target="tpu_custom_call" | custom-call | tf_op jit(solution)/shard_map/pallas_call | solution.py:407
  94.3 38.3 %shard_map.48 = bf16[4,2048,128]{2,1,0:T(8,128)(2,1)} custom-call(bf16[4,2048,128]{2,1,0:T(8,128)(2,1)} %bitcast.8, bf16[512,128]{1,0:T(8,128)(2,1)} %bitcast.10), custom_call_target="tpu_custom_call" | custom-call | tf_op jit(solution)/shard_map/pallas_call | solution.py:454
  132.6 3.0 %copy.7 = bf16[1,8192,128]{2,1,0:T(8,128)(2,1)} copy(bf16[1,8192,128]{2,1,0:T(8,128)(2,1)} %bitcast.6) | data formatting | bytes 4194304
where the time goes:
time: 136 us
  Pallas kernels  132 us (97%)
  local copies, waits for them, and re-layouts  3.05 us (2%)
    pallas_call x1, Pallas kernels, front(): pl.pallas_call(functools.partial(front_kernel, cases, tiles), out_shape=(...  68.1 us
    pallas_call x1, Pallas kernels, back(): pl.pallas_call(functools.partial(back_kernel, cases), out_shape=jax.Shape...  38.3 us
    pallas_call x1, Pallas kernels, solve(): pl.pallas_call(functools.partial(solve_kernel, cells), out_shape=jax.Shap...  25.5 us
    unnamed x1, local copies, waits for them, and re-layouts  3.05 us

commit v1 on v0

--- a/solution.py
+++ b/solution.py
@@ -12,7 +12,7 @@
 LEVELS = 2
 PAD = 8
 PANEL = 16
-GROUP = 4
+GROUP = 8
 HIGHEST = lax.Precision.HIGHEST
 MESH = pl.DeviceIdType.MESH
 VMEM_BYTES = 60 * 2**20
@@ -168,7 +168,9 @@
         lax.fori_loop(low, high, one, 0)
 
     weight = jnp.sqrt(jnp.full((1, lanes), weight_ref[0].astype(jnp.float32)))
-    copies = []
+    def row_copy(k, i):
+        return remote(out.at[k, i], s_ref.at[case, i], s_send.at[k, i], s_recv.at[k, i], case_peers[k])
+
     for k in [k for k in range(cases) if k] + [0]:
         turn = lax.rem(case + k, cases)
         first = turn * quarter
@@ -186,12 +188,12 @@
                 else:
                     s_ref[case, i, pl.ds(y, chunk)] = value
 
-        if k:
-            copy = remote(out.at[k], s_ref.at[case], s_send.at[k], s_recv.at[k], case_peers[k])
-            copy.start()
-            copies.append(copy)
-    for copy in copies:
-        copy.wait()
+            if k:
+                row_copy(k, i).start()
+
+    for i in range(quarter):
+        for k in range(1, cases):
+            row_copy(k, i).wait()
 
     block = 0
     snaps = [s_ref[g].reshape(quarter * ny, lanes) for g in range(cases)]
@@ -272,7 +274,7 @@
             pltpu.VMEM((half, share, lanes), f32),
             dma((2,)), dma((2,)),
             dma((2,)), dma((2,)),
-            dma((cases,)), dma((cases,)),
+            dma((cases, quarter)), dma((cases, quarter)),
             dma((2,)), dma((2,)),
             dma((cases,)), dma((cases,)),
             dma((half,)), dma((half,)),
@@ -332,7 +334,7 @@
 
 
 def solve_kernel(cells, gram_ref, code_ref, out_ref, full, work):
-    cases, lanes = out_ref.shape[0], out_ref.shape[2]
+    cases, lanes = out_ref.shape[1:3]
     case = lax.axis_index("case")
     block = 0
     for g in range(cases):
@@ -344,7 +346,7 @@
             block += 1
     groups = [jnp.bitwise_xor(case, g) for g in range(cases)]
     grams = {(g, h): full[groups[g], groups[h]] for g in range(cases) for h in range(cases)}
-    chains = [[0]]
+    chains = [[0, 2 ** (LEVELS - 1)]]
     for level in range(LEVELS - 1, 0, -1):
         chains.insert(0, sorted({c ^ bit for c in chains[0] for bit in (0, 2**level)}))
 
@@ -396,9 +398,10 @@
                     jnp.concatenate([dot(bases[c][1], head), dot(bases[p][1], tail)], 0),
                 )
         bases = updated
-    members, matrix = bases[0]
-    for i, g in enumerate(members):
-        out_ref[groups[g]] = matrix[i * lanes : (i + 1) * lanes].astype(out_ref.dtype)
+    for slot, c in enumerate(chains[-1]):
+        members, matrix = bases[c]
+        for i, g in enumerate(members):
+            out_ref[slot, groups[g]] = matrix[i * lanes : (i + 1) * lanes].astype(out_ref.dtype)
 
 
 def solve(cases, cells, grams, codes):
@@ -406,7 +409,7 @@
     vmem = pl.BlockSpec(memory_space=pltpu.VMEM)
     return pl.pallas_call(
         functools.partial(solve_kernel, cells),
-        out_shape=jax.ShapeDtypeStruct((cases, lanes, lanes), jnp.bfloat16),
+        out_shape=jax.ShapeDtypeStruct((2, cases, lanes, lanes), jnp.bfloat16),
         in_specs=[vmem] * 2,
         out_specs=vmem,
         scratch_shapes=[
@@ -418,33 +421,48 @@
 
 
 def back_kernel(cases, s_ref, m_ref, out_ref, buffer, m_in, send, recv, m_send, m_recv):
-    case = lax.axis_index("case")
-    case_peers = peers("case", cases)
+    case, tile = lax.axis_index("case"), lax.axis_index("tile")
+    core = lax.rem(tile, 2)
     cells = s_ref.shape[1]
     pieces = send.shape[1]
     chunk = cells // pieces
-    barrier(("case", cases))
-    copies = [remote(m_ref, m_in.at[k], m_send.at[k], m_recv.at[k], case_peers[k]) for k in range(1, cases)]
-    for copy in copies:
+    beside = case + 1 - 2 * lax.rem(case, 2)
+    devices = [{"case": lax.rem(case + cases // 2, cases)}, {"case": beside}, {"case": lax.rem(beside + cases // 2, cases)}]
+    twin = {"tile": tile + 1 - 2 * core}
+    sem = pltpu.get_barrier_semaphore()
+    for device in devices + [twin]:
+        pl.semaphore_signal(sem, inc=1, device_id=device, device_id_type=MESH)
+    pl.semaphore_wait(sem, len(devices) + 1)
+
+    depth = m_ref.shape[1] // 2
+    part = pl.ds(pl.multiple_of(core * depth, depth), depth)
+    across = remote(m_ref.at[:, part], m_in.at[:, part], m_send.at[0], m_recv.at[0], devices[1])
+    swap = remote(m_in.at[:, part], m_in.at[:, part], m_send.at[1], m_recv.at[1], twin)
+    across.start()
+
+    def product(i, matrix):
+        left = jnp.concatenate([s_ref[g, pl.ds(i * chunk, chunk), :] for g in range(cases)], 1)
+        return jnp.dot(left, matrix, preferred_element_type=jnp.float32).astype(out_ref.dtype)
+
+    copies = []
+
+    def deliver(i, k, matrix):
+        at = pl.ds(i * chunk, chunk)
+        buffer[k, at, :] = product(i, matrix)
+        copy = remote(buffer.at[k, at], out_ref.at[case, at], send.at[k, i], recv.at[k, i], devices[k])
         copy.start()
-
-    def product(i, matrix):
-        at = pl.ds(i * chunk, chunk)
-        left = jnp.concatenate([s_ref[g, at, :] for g in range(cases)], 1)
-        return jnp.dot(left, matrix, preferred_element_type=jnp.float32).astype(out_ref.dtype)
+        copies.append(copy)
 
     for i in range(pieces):
-        out_ref[case, pl.ds(i * chunk, chunk), :] = product(i, m_ref[...])
-    for copy in copies:
-        copy.wait()
-    copies = []
+        deliver(i, 0, m_ref[1])
+    across.wait()
+    swap.start()
     for i in range(pieces):
-        at = pl.ds(i * chunk, chunk)
-        for k in range(1, cases):
-            buffer[k, at, :] = product(i, m_in[cases - k])
-            copy = remote(buffer.at[k, at], out_ref.at[case, at], send.at[k, i], recv.at[k, i], case_peers[k])
-            copy.start()
-            copies.append(copy)
+        out_ref[case, pl.ds(i * chunk, chunk), :] = product(i, m_ref[0])
+    swap.wait()
+    for i in range(pieces):
+        for k in (1, 2):
+            deliver(i, k, m_in[k - 1])
     for copy in copies:
         copy.wait()
 
@@ -458,11 +476,11 @@
         out_specs=vmem,
         scratch_shapes=[
             pltpu.VMEM(snaps.shape, jnp.bfloat16),
-            pltpu.VMEM((cases,) + matrices.shape, jnp.bfloat16),
+            pltpu.VMEM(matrices.shape, jnp.bfloat16),
             pltpu.SemaphoreType.DMA((cases, 4)),
             pltpu.SemaphoreType.DMA((cases, 4)),
-            pltpu.SemaphoreType.DMA((cases,)),
-            pltpu.SemaphoreType.DMA((cases,)),
+            pltpu.SemaphoreType.DMA((2,)),
+            pltpu.SemaphoreType.DMA((2,)),
         ],
         compiler_params=pltpu.CompilerParams(collective_id=1, has_side_effects=True, vmem_limit_bytes=VMEM_BYTES),
     )(snaps, matrices)
@@ -473,7 +491,7 @@
     snaps, grams = front(cases, tiles, forcing[0], permeability[0], merge_weights)
     cells = rows * tiles * ny
     matrices = solve(cases, cells, grams.reshape(-1, lanes, lanes), start_codes)
-    basis = back(cases, snaps.reshape(cases, -1, lanes), matrices.reshape(-1, lanes))
+    basis = back(cases, snaps.reshape(cases, -1, lanes), matrices.reshape(2, -1, lanes))
     return basis.reshape(1, -1, lanes)
 
 

time: 136 us -> 133 us (0.978)
  Pallas kernels: 132 us -> 129 us
    pallas_call x1, Pallas kernels: 38.3 us -> 36.5 us  [back(): pl.pallas_call(functools.partial(back_kernel, cases), out_shape=jax.Shape...]
where the time goes in v1:
time: 133 us
  Pallas kernels  129 us (97%)
  local copies, waits for them, and re-layouts  3.05 us (2%)
    pallas_call x1, Pallas kernels, front(): pl.pallas_call(functools.partial(front_kernel, cases, tiles), out_shape=(...  67.9 us
    pallas_call x1, Pallas kernels, back(): pl.pallas_call(functools.partial(back_kernel, cases), out_shape=jax.Shape...  36.5 us
    pallas_call x1, Pallas kernels, solve(): pl.pallas_call(functools.partial(solve_kernel, cells), out_shape=jax.Shap...  25 us
    unnamed x1, local copies, waits for them, and re-layouts  3.05 us

profile of v1, /device:TPU:0, one launch (start us, length us, event | category | flops | bytes accessed | tf_op | source)
XLA Modules:
  0.0 133.1 jit_solution(8734901051321694468)
XLA Ops:
  0.7 67.9 %shard_map.46 = (bf16[4,4,512,128]{3,2,1,0:T(8,128)(2,1)}, f32[2,4,4,40,128]{4,3,2,1,0:T(8,128)}) custom-call(bf16[16,512,128]{2,1,0:T(8,128)(2,1)} %bitcast.7, f32[16,512]{1,0:T(8,128)} %bitcast.11, s32[1]{0:T(128)S(6)} %copy.6.weight_ref), custom_call_target="tpu_custom_call" | custom-call | tf_op jit(solution)/shard_map/pallas_call | solution.py:252
  68.6 25.0 %shard_map.47 = bf16[2,4,128,128]{3,2,1,0:T(8,128)(2,1)} custom-call(f32[10,128,128]{2,1,0:T(8,128)} %bitcast.10, s32[2,256,128]{2,1,0:T(8,128)} %code_ref.1), custom_call_target="tpu_custom_call" | custom-call | tf_op jit(solution)/shard_map/pallas_call | solution.py:410
  93.6 36.5 %shard_map.48 = bf16[4,2048,128]{2,1,0:T(8,128)(2,1)} custom-call(bf16[4,2048,128]{2,1,0:T(8,128)(2,1)} %bitcast.8, bf16[2,512,128]{2,1,0:T(8,128)(2,1)} %bitcast.9), custom_call_target="tpu_custom_call" | custom-call | tf_op jit(solution)/shard_map/pallas_call | solution.py:472
  130.1 3.0 %copy.7 = bf16[1,8192,128]{2,1,0:T(8,128)(2,1)} copy(bf16[1,8192,128]{2,1,0:T(8,128)(2,1)} %bitcast.6) | data formatting | bytes 4194304

commit v2 on v1

--- a/solution.py
+++ b/solution.py
@@ -11,7 +11,7 @@
 STEPS = 3
 LEVELS = 2
 PAD = 8
-PANEL = 16
+PANEL = 32
 GROUP = 8
 HIGHEST = lax.Precision.HIGHEST
 MESH = pl.DeviceIdType.MESH

time: 133 us -> 131 us (0.985)
  Pallas kernels: 129 us -> 127 us
    pallas_call x1, Pallas kernels: 25 us -> 22.7 us  [solve(): pl.pallas_call(functools.partial(solve_kernel, cells), out_shape=jax.Shap...]
where the time goes in v2:
time: 131 us
  Pallas kernels  127 us (97%)
  local copies, waits for them, and re-layouts  3.05 us (2%)
    pallas_call x1, Pallas kernels, front(): pl.pallas_call(functools.partial(front_kernel, cases, tiles), out_shape=(...  67.9 us
    pallas_call x1, Pallas kernels, back(): pl.pallas_call(functools.partial(back_kernel, cases), out_shape=jax.Shape...  36.5 us
    pallas_call x1, Pallas kernels, solve(): pl.pallas_call(functools.partial(solve_kernel, cells), out_shape=jax.Shap...  22.7 us
    unnamed x1, local copies, waits for them, and re-layouts  3.05 us

profile of v2, /device:TPU:0, one launch (start us, length us, event | category | flops | bytes accessed | tf_op | source)
XLA Modules:
  0.0 130.8 jit_solution(9300530984078724034)
XLA Ops:
  0.7 67.9 %shard_map.46 = (bf16[4,4,512,128]{3,2,1,0:T(8,128)(2,1)}, f32[2,4,4,40,128]{4,3,2,1,0:T(8,128)}) custom-call(bf16[16,512,128]{2,1,0:T(8,128)(2,1)} %bitcast.7, f32[16,512]{1,0:T(8,128)} %bitcast.11, s32[1]{0:T(128)S(6)} %copy.6.weight_ref), custom_call_target="tpu_custom_call" | custom-call | tf_op jit(solution)/shard_map/pallas_call | solution.py:252
  68.6 22.7 %shard_map.47 = bf16[2,4,128,128]{3,2,1,0:T(8,128)(2,1)} custom-call(f32[10,128,128]{2,1,0:T(8,128)} %bitcast.10, s32[2,256,128]{2,1,0:T(8,128)} %code_ref.1), custom_call_target="tpu_custom_call" | custom-call | tf_op jit(solution)/shard_map/pallas_call | solution.py:410
  91.3 36.5 %shard_map.48 = bf16[4,2048,128]{2,1,0:T(8,128)(2,1)} custom-call(bf16[4,2048,128]{2,1,0:T(8,128)(2,1)} %bitcast.8, bf16[2,512,128]{2,1,0:T(8,128)(2,1)} %bitcast.9), custom_call_target="tpu_custom_call" | custom-call | tf_op jit(solution)/shard_map/pallas_call | solution.py:472
  127.8 3.0 %copy.7 = bf16[1,8192,128]{2,1,0:T(8,128)(2,1)} copy(bf16[1,8192,128]{2,1,0:T(8,128)(2,1)} %bitcast.6) | data formatting | bytes 4194304

commit v3 on v2

--- a/solution.py
+++ b/solution.py
@@ -12,7 +12,7 @@
 LEVELS = 2
 PAD = 8
 PANEL = 32
-GROUP = 8
+GROUP = 16
 HIGHEST = lax.Precision.HIGHEST
 MESH = pl.DeviceIdType.MESH
 VMEM_BYTES = 60 * 2**20

time: 131 us -> 131 us (level)
  no operation moved by 1% of the time
where the time goes in v3:
time: 131 us
  Pallas kernels  127 us (97%)
  local copies, waits for them, and re-layouts  3.05 us (2%)
    pallas_call x1, Pallas kernels, front(): pl.pallas_call(functools.partial(front_kernel, cases, tiles), out_shape=(...  67.9 us
    pallas_call x1, Pallas kernels, back(): pl.pallas_call(functools.partial(back_kernel, cases), out_shape=jax.Shape...  36.5 us
    pallas_call x1, Pallas kernels, solve(): pl.pallas_call(functools.partial(solve_kernel, cells), out_shape=jax.Shap...  22.8 us
    unnamed x1, local copies, waits for them, and re-layouts  3.05 us

profile of v3, /device:TPU:0, one launch (start us, length us, event | category | flops | bytes accessed | tf_op | source)
XLA Modules:
  0.0 130.9 jit_solution(5038625836494233565)
XLA Ops:
  0.7 67.9 %shard_map.46 = (bf16[4,4,512,128]{3,2,1,0:T(8,128)(2,1)}, f32[2,4,4,40,128]{4,3,2,1,0:T(8,128)}) custom-call(bf16[16,512,128]{2,1,0:T(8,128)(2,1)} %bitcast.7, f32[16,512]{1,0:T(8,128)} %bitcast.11, s32[1]{0:T(128)S(6)} %copy.6.weight_ref), custom_call_target="tpu_custom_call" | custom-call | tf_op jit(solution)/shard_map/pallas_call | solution.py:252
  68.6 22.8 %shard_map.47 = bf16[2,4,128,128]{3,2,1,0:T(8,128)(2,1)} custom-call(f32[10,128,128]{2,1,0:T(8,128)} %bitcast.10, s32[2,256,128]{2,1,0:T(8,128)} %code_ref.1), custom_call_target="tpu_custom_call" | custom-call | tf_op jit(solution)/shard_map/pallas_call | solution.py:410
  91.4 36.5 %shard_map.48 = bf16[4,2048,128]{2,1,0:T(8,128)(2,1)} custom-call(bf16[4,2048,128]{2,1,0:T(8,128)(2,1)} %bitcast.8, bf16[2,512,128]{2,1,0:T(8,128)(2,1)} %bitcast.9), custom_call_target="tpu_custom_call" | custom-call | tf_op jit(solution)/shard_map/pallas_call | solution.py:472
  127.9 3.0 %copy.7 = bf16[1,8192,128]{2,1,0:T(8,128)(2,1)} copy(bf16[1,8192,128]{2,1,0:T(8,128)(2,1)} %bitcast.6) | data formatting | bytes 4194304
